TPU v7x, 32 devices: a whole 2x2x4 slice. The times are simulated.
32 devices in a mesh: job: 2 (over y), tile: 4 (over z), src: 4 (over x, core).
Axes of the slice: x: 2, y: 2, z: 4, core: 2. Of those that a mesh axis runs over, the one named last changes fastest.
Arguments:
- forward_field: float32 [8, 2, 16, 256, 128], P(('job', 'src'), None, 'tile'), parts along dimension 0, may hold values from -6 to 6
- adjoint_guess: float32 [8, 2, 16, 256, 128], P(('job', 'src'), None, 'tile'), parts along dimension 0, may hold values from -6 to 6
- conductivity: float32 [32, 256, 128], P(('job', 'tile')), parts along dimension 0, may hold values from 0.3 to 3
- freq_kappa: float32 [8], P('job'), parts along dimension 0, may hold values from 0.5 to 4
- pair_freq: int32 [8], P(('job', 'src')), parts along dimension 0, may hold values from 0 to 3
- recv_data: float32 [8, 2, 256], P(('job', 'src')), parts along dimension 0, may hold values from -6 to 6
- recv_weights: float32 [512, 64], P('job'), parts along dimension 0, may hold values from 0.05 to 1
- recv_x: int32 [512], P('job'), parts along dimension 0, may hold values from 0 to 12
- recv_y: int32 [512], P('job'), parts along dimension 0, may hold values from 0 to 252
- recv_z: int32 [512], P('job'), parts along dimension 0, may hold values from 0 to 124
Outputs:
- adjoint: float32 [8, 2, 16, 256, 128], P(('job', 'src'), None, 'tile'), parts along dimension 0
- gradient: float32 [32, 256, 128], P(('job', 'tile'), 'src'), parts along dimension 0
There are 2 independent parts, one for each index of `job`. A program takes and returns all parts, laid end to end along the dimension named above; each array names one. Nothing has to cross between parts.
Inputs may be any that keep to these rules, and one draw needn't show every extreme that they name: `recv_x`: each receiver's block of 4 x 4 x 4 cells lies inside the grid along the first dimension. `recv_y`: each receiver's block lies inside the grid along the second dimension. `recv_z`: each receiver's block lies inside the grid along the third dimension. `pair_freq`: an index into freq_kappa.
All inputs are finite; a program needn't handle non-finite values.
Results may differ from a plain program's by a relative error of at most 0.00011.
Values sent between devices are 32-bit elements; how exact they have to be, the bound alone decides.
A program may use at most 64 MiB of HBM per device.

v0:
```python
import jax
import jax.numpy as jnp
from jax import lax
from jax.sharding import PartitionSpec as P


def with_halo(cells, sides, width):
    for axis, dim in sides:
        count = lax.axis_size(axis)
        ends = count - 1
        head = lax.slice_in_dim(cells, 0, width, axis=dim)
        tail = lax.slice_in_dim(cells, cells.shape[dim] - width, cells.shape[dim], axis=dim)
        cells = jnp.concatenate(
            [
                lax.ppermute(tail, axis, [(i, (i + 1) % count) for i in range(ends)]),
                cells,
                lax.ppermute(head, axis, [((i + 1) % count, i) for i in range(ends)]),
            ],
            axis=dim,
        )
    return cells


def neighbour_update(extended, source, coupling, denominator, update_mask):
    inner = extended[:, :, 1:-1]
    padded = jnp.pad(inner, ((0, 0), (0, 0), (0, 0), (1, 1), (1, 1)))
    beside_all = extended[:, :, 2:] + extended[:, :, :-2]
    beside_all = beside_all + padded[:, :, :, 2:, 1:-1] + padded[:, :, :, :-2, 1:-1]
    beside_all = beside_all + padded[:, :, :, 1:-1, 2:] + padded[:, :, :, 1:-1, :-2]
    sums = source + beside_all
    real_part = (6.0 * sums[:, 0] + coupling * sums[:, 1]) / denominator
    imag_part = (6.0 * sums[:, 1] - coupling * sums[:, 0]) / denominator
    return jnp.where(update_mask[None, None], jnp.stack([real_part, imag_part], axis=1), inner)


def local_source(recv_data, recv_weights, recv_x, recv_y, recv_z, start_x, layers, size_y, size_z):
    recv_count = recv_weights.shape[0]
    pair_count = recv_data.shape[0]
    steps_four = jnp.arange(4, dtype=jnp.int32)
    rows_y = jnp.arange(size_y, dtype=jnp.int32)
    row_match = (
        (rows_y[:, None, None] == recv_y[None, :, None] + steps_four[None, None, :])
        .astype(jnp.float32)
        .reshape(size_y, recv_count * 4)
    )
    cols_z = jnp.arange(size_z, dtype=jnp.int32)
    col_match = (cols_z[None, None, :] == recv_z[:, None, None] + steps_four[None, :, None]).astype(
        jnp.float32
    )
    weight_block = recv_weights.reshape(recv_count, 4, 4, 4)

    def one_layer(layer):
        offset_x = start_x + layer - recv_x
        pick = (offset_x[:, None] == steps_four[None, :]).astype(jnp.float32)
        plane = jnp.sum(pick[:, :, None, None] * weight_block, axis=1)
        spread = jnp.einsum("rbk,rkz->rbz", plane, col_match, precision=lax.Precision.HIGHEST)
        scaled = (recv_data[:, :, :, None, None] * spread[None, None]).reshape(
            pair_count, 2, recv_count * 4, size_z
        )
        return jnp.einsum("ym,pcmz->pcyz", row_match, scaled, precision=lax.Precision.HIGHEST)

    stacked = lax.map(one_layer, jnp.arange(layers, dtype=jnp.int32))
    return jnp.moveaxis(stacked, 0, 2)


def colour_table(start_x, layers, size_y, size_z):
    along_x = start_x + jnp.arange(layers, dtype=jnp.int32)
    return (
        along_x[:, None, None]
        + jnp.arange(size_y, dtype=jnp.int32)[None, :, None]
        + jnp.arange(size_z, dtype=jnp.int32)[None, None, :]
    ) % 2


def body(
    forward_field,
    adjoint_guess,
    conductivity,
    freq_kappa,
    pair_freq,
    recv_data,
    recv_weights,
    recv_x,
    recv_y,
    recv_z,
):
    pair_count, parts, layers_dev, size_y, size_z = adjoint_guess.shape
    first_x = lax.axis_index("tile") * layers_dev
    freq_count = freq_kappa.shape[0]
    kappa = jnp.sum(
        jnp.where(
            pair_freq[:, None] == jnp.arange(freq_count, dtype=jnp.int32)[None, :],
            freq_kappa[None, :],
            0.0,
        ),
        axis=1,
    )
    coupling = kappa[:, None, None, None] * conductivity[None]
    denominator = 36.0 + coupling * coupling
    source = local_source(
        recv_data, recv_weights, recv_x, recv_y, recv_z, first_x, layers_dev, size_y, size_z
    )
    colours = colour_table(first_x, layers_dev, size_y, size_z)
    field = adjoint_guess
    for colour in (0, 1, 0, 1):
        extended = with_halo(field, (("tile", 2),), 1)
        field = neighbour_update(extended, source, coupling, denominator, colours == colour)
    products = forward_field[:, 0] * field[:, 1] + forward_field[:, 1] * field[:, 0]
    partial_terms = -conductivity * jnp.sum(kappa[:, None, None, None] * products, axis=0)
    gradient = lax.psum_scatter(partial_terms, "src", scatter_dimension=1, tiled=True)
    return (field, gradient)


def solution(mesh):
    placed = (
        P(("job", "src"), None, "tile", None, None),
        P(("job", "src"), None, "tile", None, None),
        P(("job", "tile"), None, None),
        P("job"),
        P(("job", "src")),
        P(("job", "src"), None, None),
        P("job", None),
        P("job"),
        P("job"),
        P("job"),
    )
    return jax.shard_map(
        body,
        mesh=mesh,
        in_specs=placed,
        out_specs=(P(("job", "src"), None, "tile", None, None), P(("job", "tile"), "src", None)),
        check_vma=False,
    )
```

profile of v0, /device:TPU:0, one launch (start us, length us, event | category | flops | bytes accessed | tf_op | source)
XLA Modules:
  0.0 113.9 jit_solution(8431818215590295439)
XLA Ops:
  7.3 1.9 %fusion.49 = (f32[1,2,1,256,128]{4,3,2,1,0:T(8,128)}, f32[1,2,1,256,128]{4,3,2,1,0:T(8,128)}) fusion(f32[1,2,4,256,128]{4,3,2,1,0:T(8,128)} %param.13), kind=kLoop, calls=%fused_computation.110 | loop fusion | bytes 1048576 | tf_op jit(solution)/shard_map/slice | solution.py:11
  9.1 1.3 %collective-permute-start = (f32[1,2,1,256,128]{4,3,2,1,0:T(8,128)}, f32[1,2,1,256,128]{4,3,2,1,0:T(8,128)}, u32[]{:S(2)}, u32[]{:S(2)}) collective-permute-start(f32[1,2,1,256,128]{4,3,2,1,0:T(8,128)} %get-tuple-element.154), channel_id=1, source_target_pairs={{4,0},{8,4},{12,8},{5,1},{9,5},{13,9},{6,2},{10,6},{14,10},{7,3},{... | collective-permute-start | bytes 786440 | tf_op jit(solution)/shard_map/ppermute | solution.py:17
  10.4 6.3 %collective-permute-start.1 = (f32[1,2,1,256,128]{4,3,2,1,0:T(8,128)}, f32[1,2,1,256,128]{4,3,2,1,0:T(8,128)}, u32[]{:S(2)}, u32[]{:S(2)}) collective-permute-start(f32[1,2,1,256,128]{4,3,2,1,0:T(8,128)} %get-tuple-element.155), channel_id=1, source_target_pairs={{0,4},{4,8},{8,12},{1,5},{5,9},{9,13},{2,6},{6,10},{10,14},{3,7},{... | collective-permute-start | bytes 786440 | tf_op jit(solution)/shard_map/ppermute | solution.py:15
  18.0 21.1 %while.13 = (s32[]{:T(128)}, f32[4,1,2,256,128]{4,3,0,2,1:T(8,128)S(1)}, f32[1,2,256]{2,1,0:T(2,128)S(1)}, s32[4]{0:T(128)S(1)}, s32[]{:T(128)}, /*index=5*/s32[...) while((s32[]{:T(128)}, ...), condition=%wide.region_2.3_spmd.clone.clone, body=%wide.region_0.0_spmd.clone.clone.sunk | while | flops 812677376 | bytes 3593373 | solution.py:62
  18.0 0.6 dynamic_slice.8
  19.3 0.1 mul.291
  19.5 0.2 mul.292
  19.6 0.3 copy.29
  19.9 1.9 %fusion.60 = f32[256,4,128]{2,1,0:T(4,128)S(1)} fusion(f32[256,4,4]{2,1,0:T(4,128)S(1)} %copy.29, s32[256,4]{1,0:T(8,128)S(1)} %get-tuple-element.240), kind=kOutput, calls=%fused_computation.8.clone.1 | convolution fusion | flops 6553600 | bytes 544768 | tf_op jit(solution)/shard_map/while/body/eval_jaxpr/rbk,rkz->rbz/dot_general | solution.py:56
  21.8 0.2 copy.30
  22.0 1.1 convolution_bitcast_fusion.2
  23.1 0.1 copy.31
  23.3 0.6 dynamic_slice.8
  24.6 0.1 mul.291
  24.7 0.2 mul.292
  24.9 0.3 copy.29
  25.2 1.9 %fusion.60 = f32[256,4,128]{2,1,0:T(4,128)S(1)} fusion(f32[256,4,4]{2,1,0:T(4,128)S(1)} %copy.29, s32[256,4]{1,0:T(8,128)S(1)} %get-tuple-element.240), kind=kOutput, calls=%fused_computation.8.clone.1 | convolution fusion | flops 6553600 | bytes 544768 | tf_op jit(solution)/shard_map/while/body/eval_jaxpr/rbk,rkz->rbz/dot_general | solution.py:56
  27.1 0.2 copy.30
  27.3 1.1 convolution_bitcast_fusion.2
  28.4 0.1 copy.31
  28.6 0.6 dynamic_slice.8
  29.9 0.1 mul.291
  30.0 0.2 mul.292
  30.2 0.3 copy.29
  30.5 1.9 %fusion.60 = f32[256,4,128]{2,1,0:T(4,128)S(1)} fusion(f32[256,4,4]{2,1,0:T(4,128)S(1)} %copy.29, s32[256,4]{1,0:T(8,128)S(1)} %get-tuple-element.240), kind=kOutput, calls=%fused_computation.8.clone.1 | convolution fusion | flops 6553600 | bytes 544768 | tf_op jit(solution)/shard_map/while/body/eval_jaxpr/rbk,rkz->rbz/dot_general | solution.py:56
  32.3 0.2 copy.30
  32.5 1.1 convolution_bitcast_fusion.2
  33.7 0.1 copy.31
  33.8 0.6 dynamic_slice.8
  35.2 0.1 mul.291
  35.3 0.2 mul.292
  35.5 0.3 copy.29
  35.8 1.9 %fusion.60 = f32[256,4,128]{2,1,0:T(4,128)S(1)} fusion(f32[256,4,4]{2,1,0:T(4,128)S(1)} %copy.29, s32[256,4]{1,0:T(8,128)S(1)} %get-tuple-element.240), kind=kOutput, calls=%fused_computation.8.clone.1 | convolution fusion | flops 6553600 | bytes 544768 | tf_op jit(solution)/shard_map/while/body/eval_jaxpr/rbk,rkz->rbz/dot_general | solution.py:56
  37.6 0.2 copy.30
  37.8 1.1 convolution_bitcast_fusion.2
  39.0 0.1 copy.31
  39.1 0.6 fusion.45
  39.7 0.4 broadcast_compare_fusion
  40.2 1.7 %fusion.17 = f32[1,2,4,256,128]{4,3,2,1,0:T(8,128)S(1)} fusion(f32[1,2,4,256,128]{4,3,2,1,0:T(8,128)S(1)} %copy-done, f32[1,2,1,256,128]{4,3,2,1,0:T(8,128)} %collective-permute-done.1, f32[1,2,1,256,128]{4,3,2,1,0:T(8,128)} %collective-permute-done, f32[4,1,2,256,128]{4,3,0,2,1:T(8,128)S(1)} %get-tuple-element.76), kind=kLoop, calls=%fused_computation.38 | loop fusion | flops 2097152 | bytes 3670016 | tf_op jit(solution)/shard_map/add | solution.py:30
  41.9 0.9 divide_bitcast_fusion.7
  42.9 1.3 %collective-permute-start.2 = (f32[1,2,1,256,128]{4,3,2,1,0:T(8,128)S(1)}, f32[1,2,1,256,128]{4,3,2,1,0:T(8,128)S(1)}, u32[]{:S(2)}, u32[]{:S(2)}) collective-permute-start(f32[1,2,1,256,128]{4,3,2,1,0:T(8,128)S(1)} %get-tuple-element.152), channel_id=1, source_target_pairs={{4,0},{8,4},{12,8},{5,1},{9,5},{13,9},{6,2},{10,6},{14,10},{7,3},{... | collective-permute-start | bytes 786440 | tf_op jit(solution)/shard_map/ppermute | solution.py:17
  44.2 4.6 %collective-permute-start.3 = (f32[1,2,1,256,128]{4,3,2,1,0:T(8,128)S(1)}, f32[1,2,1,256,128]{4,3,2,1,0:T(8,128)S(1)}, u32[]{:S(2)}, u32[]{:S(2)}) collective-permute-start(f32[1,2,1,256,128]{4,3,2,1,0:T(8,128)S(1)} %get-tuple-element.153), channel_id=1, source_target_pairs={{0,4},{4,8},{8,12},{1,5},{5,9},{9,13},{2,6},{6,10},{10,14},{3,7},{... | collective-permute-start | bytes 786440 | tf_op jit(solution)/shard_map/ppermute | solution.py:15
  48.8 3.8 %collective-permute-done.2 = f32[1,2,1,256,128]{4,3,2,1,0:T(8,128)S(1)} collective-permute-done((f32[1,2,1,256,128]{4,3,2,1,0:T(8,128)S(1)}, f32[1,2,1,256,128]{4,3,2,1,0:T(8,128)S(1)}, u32[]{:S(2)}, u32[]{:S(2)}) %collective-permute-start.2) | collective-permute-done | bytes 262176 | tf_op jit(solution)/shard_map/ppermute | solution.py:17
  52.6 1.2 %collective-permute-done.3 = f32[1,2,1,256,128]{4,3,2,1,0:T(8,128)S(1)} collective-permute-done((f32[1,2,1,256,128]{4,3,2,1,0:T(8,128)S(1)}, f32[1,2,1,256,128]{4,3,2,1,0:T(8,128)S(1)}, u32[]{:S(2)}, u32[]{:S(2)}) %collective-permute-start.3) | collective-permute-done | bytes 262176 | tf_op jit(solution)/shard_map/ppermute | solution.py:15
  53.8 0.6 fusion.22
  54.4 0.9 divide_bitcast_fusion.5
  55.3 0.2 maximum_select_fusion.1
  55.5 1.3 %collective-permute-start.4 = (f32[1,2,1,256,128]{4,3,2,1,0:T(8,128)S(1)}, f32[1,2,1,256,128]{4,3,2,1,0:T(8,128)S(1)}, u32[]{:S(2)}, u32[]{:S(2)}) collective-permute-start(f32[1,2,1,256,128]{4,3,2,1,0:T(8,128)S(1)} %get-tuple-element.150), channel_id=1, source_target_pairs={{4,0},{8,4},{12,8},{5,1},{9,5},{13,9},{6,2},{10,6},{14,10},{7,3},{... | collective-permute-start | bytes 786440 | tf_op jit(solution)/shard_map/ppermute | solution.py:17
  56.8 5.0 %collective-permute-start.5 = (f32[1,2,1,256,128]{4,3,2,1,0:T(8,128)S(1)}, f32[1,2,1,256,128]{4,3,2,1,0:T(8,128)S(1)}, u32[]{:S(2)}, u32[]{:S(2)}) collective-permute-start(f32[1,2,1,256,128]{4,3,2,1,0:T(8,128)S(1)} %get-tuple-element.151), channel_id=1, source_target_pairs={{0,4},{4,8},{8,12},{1,5},{5,9},{9,13},{2,6},{6,10},{10,14},{3,7},{... | collective-permute-start | bytes 786440 | tf_op jit(solution)/shard_map/ppermute | solution.py:15
  61.8 2.9 %collective-permute-done.4 = f32[1,2,1,256,128]{4,3,2,1,0:T(8,128)S(1)} collective-permute-done((f32[1,2,1,256,128]{4,3,2,1,0:T(8,128)S(1)}, f32[1,2,1,256,128]{4,3,2,1,0:T(8,128)S(1)}, u32[]{:S(2)}, u32[]{:S(2)}) %collective-permute-start.4) | collective-permute-done | bytes 262176 | tf_op jit(solution)/shard_map/ppermute | solution.py:17
  64.7 1.2 %collective-permute-done.5 = f32[1,2,1,256,128]{4,3,2,1,0:T(8,128)S(1)} collective-permute-done((f32[1,2,1,256,128]{4,3,2,1,0:T(8,128)S(1)}, f32[1,2,1,256,128]{4,3,2,1,0:T(8,128)S(1)}, u32[]{:S(2)}, u32[]{:S(2)}) %collective-permute-start.5) | collective-permute-done | bytes 262176 | tf_op jit(solution)/shard_map/ppermute | solution.py:15
  65.9 0.6 fusion.27
  66.5 0.9 divide_bitcast_fusion.3
  67.3 0.2 maximum_select_fusion.2
  67.6 1.3 %collective-permute-start.6 = (f32[1,2,1,256,128]{4,3,2,1,0:T(8,128)S(1)}, f32[1,2,1,256,128]{4,3,2,1,0:T(8,128)S(1)}, u32[]{:S(2)}, u32[]{:S(2)}) collective-permute-start(f32[1,2,1,256,128]{4,3,2,1,0:T(8,128)S(1)} %get-tuple-element.148), channel_id=1, source_target_pairs={{4,0},{8,4},{12,8},{5,1},{9,5},{13,9},{6,2},{10,6},{14,10},{7,3},{... | collective-permute-start | bytes 786440 | tf_op jit(solution)/shard_map/ppermute | solution.py:17
  68.9 5.0 %collective-permute-start.7 = (f32[1,2,1,256,128]{4,3,2,1,0:T(8,128)S(1)}, f32[1,2,1,256,128]{4,3,2,1,0:T(8,128)S(1)}, u32[]{:S(2)}, u32[]{:S(2)}) collective-permute-start(f32[1,2,1,256,128]{4,3,2,1,0:T(8,128)S(1)} %get-tuple-element.149), channel_id=1, source_target_pairs={{0,4},{4,8},{8,12},{1,5},{5,9},{9,13},{2,6},{6,10},{10,14},{3,7},{... | collective-permute-start | bytes 786440 | tf_op jit(solution)/shard_map/ppermute | solution.py:15
  74.0 2.4 %collective-permute-done.6 = f32[1,2,1,256,128]{4,3,2,1,0:T(8,128)S(1)} collective-permute-done((f32[1,2,1,256,128]{4,3,2,1,0:T(8,128)S(1)}, f32[1,2,1,256,128]{4,3,2,1,0:T(8,128)S(1)}, u32[]{:S(2)}, u32[]{:S(2)}) %collective-permute-start.6) | collective-permute-done | bytes 262176 | tf_op jit(solution)/shard_map/ppermute | solution.py:17
  76.4 1.5 %collective-permute-done.7 = f32[1,2,1,256,128]{4,3,2,1,0:T(8,128)S(1)} collective-permute-done((f32[1,2,1,256,128]{4,3,2,1,0:T(8,128)S(1)}, f32[1,2,1,256,128]{4,3,2,1,0:T(8,128)S(1)}, u32[]{:S(2)}, u32[]{:S(2)}) %collective-permute-start.7) | collective-permute-done | bytes 262176 | tf_op jit(solution)/shard_map/ppermute | solution.py:15
  77.8 0.6 fusion.32
  78.5 0.9 divide_bitcast_fusion.1
  79.3 0.3 maximum_select_fusion.3
  79.6 0.9 copy-done.3
  80.5 1.6 %fusion.41 = f32[4,256,128]{2,1,0:T(8,128)} fusion(f32[1,2,4,256,128]{4,3,2,1,0:T(8,128)S(1)} %maximum_select_fusion.3, f32[1,2,4,256,128]{4,3,2,1,0:T(8,128)S(1)} %copy-done.3, f32[4,256,128]{2,1,0:T(8,128)S(1)} %copy-done.1, f32[]{:T(128)} %fusion.45), kind=kLoop, calls=%fused_computation.78 | loop fusion | flops 786432 | bytes 3145732 | tf_op jit(solution)/shard_map/mul | solution.py:109
  82.2 24.8 %reduce-scatter.2.cloned.1.call-done = f32[4,64,128]{2,1,0:T(8,128)} async-done(((f32[4,256,128]{2,1,0:T(8,128)}), f32[4,64,128]{2,1,0:T(8,128)}) %reduce-scatter.2.cloned.1.call-update) | async-done | bytes 131088 | tf_op jit(solution)/shard_map/reduce_scatter | solution.py:110
  (54 shorter events, 1.4 us)
Async XLA Ops:
  7.2 10.2 %copy-start.4 = (f32[256,64]{0,1:T(8,128)S(1)}, f32[256,64]{0,1:T(8,128)}, u32[]{:S(2)}) copy-start(f32[256,64]{0,1:T(8,128)} %param.18) | copy-start | bytes 196612
  7.2 10.3 %copy-start.7 = (s32[256]{0:T(256)S(1)}, s32[256]{0:T(256)}, u32[]{:S(2)}) copy-start(s32[256]{0:T(256)} %param.20) | copy-start | bytes 3076
  7.2 10.5 %copy-start.8 = (s32[256]{0:T(256)S(1)}, s32[256]{0:T(256)}, u32[]{:S(2)}) copy-start(s32[256]{0:T(256)} %param.21) | copy-start | bytes 3076
  7.2 10.7 %copy-start.6 = (s32[256]{0:T(256)S(1)}, s32[256]{0:T(256)}, u32[]{:S(2)}) copy-start(s32[256]{0:T(256)} %param.19) | copy-start | bytes 3076
  7.2 10.7 %copy-start.5 = (f32[1,2,256]{2,1,0:T(2,128)S(1)}, f32[1,2,256]{2,1,0:T(2,128)}, u32[]{:S(2)}) copy-start(f32[1,2,256]{2,1,0:T(2,128)} %param.17) | copy-start | bytes 6148
  7.2 99.8 %reduce-scatter.2.cloned.1.call-start = ((), (), s32[]{:S(2)}) async-start(), calls=%async_computation.1 | async-start | bytes 655360 | tf_op jit(solution)/shard_map/reduce_scatter | solution.py:110
  9.1 31.0 %collective-permute-start = (f32[1,2,1,256,128]{4,3,2,1,0:T(8,128)}, f32[1,2,1,256,128]{4,3,2,1,0:T(8,128)}, u32[]{:S(2)}, u32[]{:S(2)}) collective-permute-start(f32[1,2,1,256,128]{4,3,2,1,0:T(8,128)} %get-tuple-element.154), channel_id=1, source_target_pairs={{4,0},{8,4},{12,8},{5,1},{9,5},{13,9},{6,2},{10,6},{14,10},{7,3},{... | collective-permute-start | bytes 786440 | tf_op jit(solution)/shard_map/ppermute | solution.py:17
  10.4 29.8 %collective-permute-start.1 = (f32[1,2,1,256,128]{4,3,2,1,0:T(8,128)}, f32[1,2,1,256,128]{4,3,2,1,0:T(8,128)}, u32[]{:S(2)}, u32[]{:S(2)}) collective-permute-start(f32[1,2,1,256,128]{4,3,2,1,0:T(8,128)} %get-tuple-element.155), channel_id=1, source_target_pairs={{0,4},{4,8},{8,12},{1,5},{5,9},{9,13},{2,6},{6,10},{10,14},{3,7},{... | collective-permute-start | bytes 786440 | tf_op jit(solution)/shard_map/ppermute | solution.py:15
  18.0 21.2 %copy-start.9 = (f32[4]{0:T(128)S(1)}, f32[4]{0:T(128)}, u32[]{:S(2)}) copy-start(f32[4]{0:T(128)} %param.15) | copy-start | bytes 52
  18.0 22.2 %copy-start = (f32[1,2,4,256,128]{4,3,2,1,0:T(8,128)S(1)}, f32[1,2,4,256,128]{4,3,2,1,0:T(8,128)}, u32[]{:S(2)}) copy-start(f32[1,2,4,256,128]{4,3,2,1,0:T(8,128)} %param.13) | copy-start | bytes 3145732
  40.2 1.7 %copy-start.1 = (f32[4,256,128]{2,1,0:T(8,128)S(1)}, f32[4,256,128]{2,1,0:T(8,128)}, u32[]{:S(2)}) copy-start(f32[4,256,128]{2,1,0:T(8,128)} %param.14) | copy-start | bytes 1572868
  42.9 9.7 %collective-permute-start.2 = (f32[1,2,1,256,128]{4,3,2,1,0:T(8,128)S(1)}, f32[1,2,1,256,128]{4,3,2,1,0:T(8,128)S(1)}, u32[]{:S(2)}, u32[]{:S(2)}) collective-permute-start(f32[1,2,1,256,128]{4,3,2,1,0:T(8,128)S(1)} %get-tuple-element.152), channel_id=1, source_target_pairs={{4,0},{8,4},{12,8},{5,1},{9,5},{13,9},{6,2},{10,6},{14,10},{7,3},{... | collective-permute-start | bytes 786440 | tf_op jit(solution)/shard_map/ppermute | solution.py:17
  44.2 9.5 %collective-permute-start.3 = (f32[1,2,1,256,128]{4,3,2,1,0:T(8,128)S(1)}, f32[1,2,1,256,128]{4,3,2,1,0:T(8,128)S(1)}, u32[]{:S(2)}, u32[]{:S(2)}) collective-permute-start(f32[1,2,1,256,128]{4,3,2,1,0:T(8,128)S(1)} %get-tuple-element.153), channel_id=1, source_target_pairs={{0,4},{4,8},{8,12},{1,5},{5,9},{9,13},{2,6},{6,10},{10,14},{3,7},{... | collective-permute-start | bytes 786440 | tf_op jit(solution)/shard_map/ppermute | solution.py:15
  55.5 9.2 %collective-permute-start.4 = (f32[1,2,1,256,128]{4,3,2,1,0:T(8,128)S(1)}, f32[1,2,1,256,128]{4,3,2,1,0:T(8,128)S(1)}, u32[]{:S(2)}, u32[]{:S(2)}) collective-permute-start(f32[1,2,1,256,128]{4,3,2,1,0:T(8,128)S(1)} %get-tuple-element.150), channel_id=1, source_target_pairs={{4,0},{8,4},{12,8},{5,1},{9,5},{13,9},{6,2},{10,6},{14,10},{7,3},{... | collective-permute-start | bytes 786440 | tf_op jit(solution)/shard_map/ppermute | solution.py:17
  56.8 9.1 %collective-permute-start.5 = (f32[1,2,1,256,128]{4,3,2,1,0:T(8,128)S(1)}, f32[1,2,1,256,128]{4,3,2,1,0:T(8,128)S(1)}, u32[]{:S(2)}, u32[]{:S(2)}) collective-permute-start(f32[1,2,1,256,128]{4,3,2,1,0:T(8,128)S(1)} %get-tuple-element.151), channel_id=1, source_target_pairs={{0,4},{4,8},{8,12},{1,5},{5,9},{9,13},{2,6},{6,10},{10,14},{3,7},{... | collective-permute-start | bytes 786440 | tf_op jit(solution)/shard_map/ppermute | solution.py:15
  67.6 8.7 %collective-permute-start.6 = (f32[1,2,1,256,128]{4,3,2,1,0:T(8,128)S(1)}, f32[1,2,1,256,128]{4,3,2,1,0:T(8,128)S(1)}, u32[]{:S(2)}, u32[]{:S(2)}) collective-permute-start(f32[1,2,1,256,128]{4,3,2,1,0:T(8,128)S(1)} %get-tuple-element.148), channel_id=1, source_target_pairs={{4,0},{8,4},{12,8},{5,1},{9,5},{13,9},{6,2},{10,6},{14,10},{7,3},{... | collective-permute-start | bytes 786440 | tf_op jit(solution)/shard_map/ppermute | solution.py:17
  68.9 8.9 %collective-permute-start.7 = (f32[1,2,1,256,128]{4,3,2,1,0:T(8,128)S(1)}, f32[1,2,1,256,128]{4,3,2,1,0:T(8,128)S(1)}, u32[]{:S(2)}, u32[]{:S(2)}) collective-permute-start(f32[1,2,1,256,128]{4,3,2,1,0:T(8,128)S(1)} %get-tuple-element.149), channel_id=1, source_target_pairs={{0,4},{4,8},{8,12},{1,5},{5,9},{9,13},{2,6},{6,10},{10,14},{3,7},{... | collective-permute-start | bytes 786440 | tf_op jit(solution)/shard_map/ppermute | solution.py:15
  79.3 1.2 %copy-start.3 = (f32[1,2,4,256,128]{4,3,2,1,0:T(8,128)S(1)}, f32[1,2,4,256,128]{4,3,2,1,0:T(8,128)}, u32[]{:S(2)}) copy-start(f32[1,2,4,256,128]{4,3,2,1,0:T(8,128)} %param.12) | copy-start | bytes 3145732
  80.5 1.6 %copy-start.2 = (f32[1,2,4,256,128]{4,3,2,1,0:T(8,128)}, f32[1,2,4,256,128]{4,3,2,1,0:T(8,128)S(1)}, u32[]{:S(2)}) copy-start(f32[1,2,4,256,128]{4,3,2,1,0:T(8,128)S(1)} %maximum_select_fusion.3) | copy-start | bytes 3145732
Sparse Core Ops, SparseCore 0:
  82.3 24.6 reduce-scatter.1
where the time goes:
time: 114 us
  waiting for transfers between devices  37.7 us (33%)
  starting transfers between devices  26.1 us (23%)
  between operations  15.1 us (13%)
  matrix products  11.9 us (10%)
  other arithmetic  11 us (10%)
  local copies, waits for them, and re-layouts  9.25 us (8%)
  loops' own time  2.83 us (2%)
    reduce_scatter x1, waiting for transfers between devices, body(): lax.psum_scatter(partial_terms, 'src', scatter_dimension=1, tiled=True)  24.8 us
    ppermute x4, starting transfers between devices, with_halo(): lax.ppermute(tail, axis, [(i, (i + 1) % count) for i in range(ends)])  20.9 us
    ppermute x4, waiting for transfers between devices, with_halo(): lax.ppermute(head, axis, [((i + 1) % count, i) for i in range(ends)])  9.05 us
    dot_general x4, matrix products, one_layer(): jnp.einsum('rbk,rkz->rbz', plane, col_match, precision=lax.Precision.HIGH...  7.46 us
    ppermute x4, starting transfers between devices, with_halo(): lax.ppermute(head, axis, [((i + 1) % count, i) for i in range(ends)])  5.16 us
    dot_general x4, matrix products, one_layer(): jnp.einsum('ym,pcmz->pcyz', row_match, scaled, precision=lax.Precision.HI...  4.46 us
    ppermute x4, waiting for transfers between devices, with_halo(): lax.ppermute(tail, axis, [(i, (i + 1) % count) for i in range(ends)])  3.82 us
    add x4, other arithmetic, neighbour_update(): sums = source + beside_all  3.52 us
  transfers between devices with their start and end apart: 9, of which 7 were waited for; matrix products, arithmetic and copies ran while one was open for 17% of the time, Pallas kernels for 0%

commit v1 on v0

v1 whole, which is shorter than its diff:
```python
import functools

import jax
import jax.numpy as jnp
from jax import lax
from jax.experimental import pallas as pl
from jax.experimental.pallas import tpu as pltpu
from jax.sharding import PartitionSpec as P

MESH = pl.DeviceIdType.MESH
PAD = 8
F32 = jnp.float32
BF16 = jnp.bfloat16


def kernel(
    tiles,
    srcs,
    freq_ref,
    kappa_ref,
    fwd_hbm,
    guess_hbm,
    cond_hbm,
    data_ref,
    weights_ref,
    rx_ref,
    ry_ref,
    rz_ref,
    adj_ref,
    grad_ref,
    guess_ref,
    fwd_ref,
    cond_ref,
    b0_ref,
    r1_ref,
    b2_ref,
    r3_ref,
    halo_ref,
    src_ref,
    c6_ref,
    cc_ref,
    rows_ref,
    cols_ref,
    g_red,
    g_in,
    g_out,
    got_red,
    got_in,
    got_out,
    load_sem,
    send_sem,
    recv_sem,
    gsend_sem,
    grecv_sem,
):
    layers, _, half, size_z = src_ref.shape[1:]
    recv_count = rx_ref.shape[1]
    chunk = half // srcs
    last = layers - 1
    tile = lax.axis_index("tile")
    me = lax.axis_index("src")
    has_left = tile > 0
    has_right = tile < tiles - 1
    left = jnp.maximum(tile - 1, 0)
    right = jnp.minimum(tile + 1, tiles - 1)
    first_x = tile * layers

    loads = []

    def load(source, target):
        copy = pltpu.make_async_copy(source, target, load_sem.at[len(loads)])
        copy.start()
        loads.append(copy)
        return copy

    edge_loads = [load(guess_hbm.at[0, :, l], guess_ref.at[:, l]) for l in (0, last)]
    cond_load = load(cond_hbm, cond_ref)
    inner_load = load(guess_hbm.at[0, :, pl.ds(1, layers - 2)], guess_ref.at[:, pl.ds(1, layers - 2)])
    fwd_load = load(fwd_hbm.at[0], fwd_ref)

    barrier = pltpu.get_barrier_semaphore()

    @pl.when(has_left)
    def _():
        pl.semaphore_signal(barrier, inc=1, device_id={"tile": left}, device_id_type=MESH)

    @pl.when(has_right)
    def _():
        pl.semaphore_signal(barrier, inc=1, device_id={"tile": right}, device_id_type=MESH)

    for step in range(1, srcs):
        pl.semaphore_signal(
            barrier, inc=1, device_id={"src": lax.rem(me + step, srcs)}, device_id_type=MESH
        )

    lane = lax.broadcasted_iota(jnp.int32, (1, size_z), 1)

    def red_odd(l):
        return ((lane + (first_x + l)) & 1) == 1

    zeros_edge = jnp.zeros((PAD, size_z), F32)
    for buf in (b0_ref, r1_ref, b2_ref, r3_ref):
        for l in range(layers):
            for c in range(2):
                buf[l, c, 0:PAD, :] = zeros_edge
                buf[l, c, PAD + half : 2 * PAD + half, :] = zeros_edge

    @pl.when(jnp.logical_not(has_left))
    def _():
        for h in range(4):
            halo_ref[h, 0] = jnp.zeros((2, half, size_z), F32)

    @pl.when(jnp.logical_not(has_right))
    def _():
        for h in range(4):
            halo_ref[h, 1] = jnp.zeros((2, half, size_z), F32)

    even = pl.ds(0, half, stride=2)
    odd = pl.ds(1, half, stride=2)

    def pack_guess(l):
        pi = red_odd(l)
        for c in range(2):
            b0_ref[l, c, PAD : PAD + half, :] = jnp.where(
                pi, guess_ref[c, l, even, :], guess_ref[c, l, odd, :]
            )

    def halo_copy(h, buf, side):
        l, to = (last, right) if side == 0 else (0, left)
        return pltpu.make_async_remote_copy(
            src_ref=buf.at[l, :, pl.ds(PAD, half), :],
            dst_ref=halo_ref.at[h, side],
            send_sem=send_sem.at[h, side],
            recv_sem=recv_sem.at[h, side],
            device_id={"tile": to},
            device_id_type=MESH,
        )

    def halo_start(h, buf, side):
        @pl.when(has_right if side == 0 else has_left)
        def _():
            halo_copy(h, buf, side).start()

    def halo_wait(h, buf, side):
        @pl.when(has_left if side == 0 else has_right)
        def _():
            halo_copy(h, buf, side).wait_recv()

    def halo_sent(h, buf, side):
        @pl.when(has_right if side == 0 else has_left)
        def _():
            halo_copy(h, buf, side).wait_send()

    for copy, l in zip(edge_loads, (0, last)):
        copy.wait()
        pack_guess(l)

    peers = has_left.astype(jnp.int32) + has_right.astype(jnp.int32) + (srcs - 1)
    pl.semaphore_wait(barrier, peers)

    for side in range(2):
        halo_start(0, b0_ref, side)

    cond_load.wait()
    freq = freq_ref[0]
    kappa = jnp.float32(0.0)
    for i in range(kappa_ref.shape[0]):
        kappa = kappa + jnp.where(freq == i, kappa_ref[i], jnp.float32(0.0))
    for l in range(layers):
        pi = red_odd(l)
        ce = cond_ref[l, even, :]
        co = cond_ref[l, odd, :]
        for k, cell in enumerate((jnp.where(pi, co, ce), jnp.where(pi, ce, co))):
            coupling = kappa * cell
            inverse = 1.0 / (36.0 + coupling * coupling)
            c6_ref[k, l] = 6.0 * inverse
            cc_ref[k, l] = coupling * inverse
    inner_load.wait()
    for l in range(1, last):
        pack_guess(l)

    ry = ry_ref[...]
    row = lax.broadcasted_iota(jnp.int32, (half, recv_count), 0) * 2
    for parity in range(2):
        for b in range(4):
            rows_ref[parity * half : (parity + 1) * half, b * recv_count : (b + 1) * recv_count] = (
                jnp.where(row + parity == ry + b, 1.0, 0.0).astype(BF16)
            )
    w_t = jnp.transpose(weights_ref[...])
    rx = rx_ref[...]
    rz = rz_ref[...]
    ZC = 16
    for l in range(layers):
        pi = red_odd(l)
        at = (first_x + l) - rx
        plane = jnp.zeros((16, recv_count), F32)
        for a in range(4):
            plane = jnp.where(at == a, w_t[16 * a : 16 * a + 16, :], plane)
        for c in range(2):
            vals = plane * data_ref[c : c + 1, :]
            for z0 in range(0, size_z, ZC):
                off = lax.broadcasted_iota(jnp.int32, (ZC, recv_count), 0) + z0 - rz
                for b in range(4):
                    t = jnp.zeros((ZC, recv_count), F32)
                    for k in range(4):
                        t = jnp.where(off == k, vals[4 * b + k : 4 * b + k + 1, :], t)
                    hi = t.astype(BF16)
                    lo = (t - hi.astype(F32)).astype(BF16)
                    cols = slice(b * recv_count, (b + 1) * recv_count)
                    cols_ref[c, z0 : z0 + ZC, cols] = hi
                    cols_ref[c, size_z + z0 : size_z + z0 + ZC, cols] = lo
            both = lax.dot_general(
                rows_ref[...],
                cols_ref[c],
                (((1,), (1,)), ((), ())),
                preferred_element_type=F32,
            )
            total = both[:, :size_z] + both[:, size_z:]
            se, so = total[:half], total[half:]
            src_ref[0, l, c] = jnp.where(pi, so, se)
            src_ref[1, l, c] = jnp.where(pi, se, so)

    RC = min(32, half)

    def update(colour, h, buf, out, out_pad, l):
        up_side = red_odd(l) if colour == 0 else jnp.logical_not(red_odd(l))
        for r in range(0, half, RC):
            sums = []
            for c in range(2):
                mid = buf[l, c, PAD + r : PAD + r + RC, :]
                s = src_ref[colour, l, c, r : r + RC, :] + mid
                s = s + jnp.where(
                    up_side,
                    buf[l, c, PAD + r + 1 : PAD + r + 1 + RC, :],
                    buf[l, c, PAD + r - 1 : PAD + r - 1 + RC, :],
                )
                if l == 0:
                    s = s + halo_ref[h, 0, c, r : r + RC, :]
                else:
                    s = s + buf[l - 1, c, PAD + r : PAD + r + RC, :]
                if l == last:
                    s = s + halo_ref[h, 1, c, r : r + RC, :]
                else:
                    s = s + buf[l + 1, c, PAD + r : PAD + r + RC, :]
                s = s + jnp.where(lane == 0, 0.0, pltpu.roll(mid, 1, 1))
                s = s + jnp.where(lane == size_z - 1, 0.0, pltpu.roll(mid, size_z - 1, 1))
                sums.append(s)
            c6 = c6_ref[colour, l, r : r + RC, :]
            cc = cc_ref[colour, l, r : r + RC, :]
            out[l, 0, out_pad + r : out_pad + r + RC, :] = c6 * sums[0] + cc * sums[1]
            out[l, 1, out_pad + r : out_pad + r + RC, :] = c6 * sums[1] - cc * sums[0]

    def sweep(colour, h, buf, out):
        for l in range(1, last):
            update(colour, h, buf, out, PAD, l)
        for side in range(2):
            halo_wait(h, buf, side)
        update(colour, h, buf, out, PAD, last)
        if h < 3:
            halo_start(h + 1, out, 0)
        update(colour, h, buf, out, PAD, 0)
        if h < 3:
            halo_start(h + 1, out, 1)

    sweep(0, 0, b0_ref, r1_ref)
    sweep(1, 1, r1_ref, b2_ref)
    sweep(0, 2, b2_ref, r3_ref)

    def terms(colour, buf, out, l, slot):
        pi = red_odd(l) if colour == 0 else jnp.logical_not(red_odd(l))
        for s in range(srcs):
            e = pl.ds(2 * s * chunk, chunk, stride=2)
            o = pl.ds(2 * s * chunk + 1, chunk, stride=2)
            fre = jnp.where(pi, fwd_ref[0, l, o, :], fwd_ref[0, l, e, :])
            fim = jnp.where(pi, fwd_ref[1, l, o, :], fwd_ref[1, l, e, :])
            cell = jnp.where(pi, cond_ref[l, o, :], cond_ref[l, e, :])
            rows = pl.ds(PAD + s * chunk, chunk)
            value = fre * buf[l, 1, rows, :] + fim * buf[l, 0, rows, :]
            out[s, slot] = (-kappa * cell) * value

    def grad_copies(group, terms_ref, got_ref):
        copies = []
        for step in range(1, srcs):
            to = lax.rem(me + step, srcs)
            copies.append(
                pltpu.make_async_remote_copy(
                    src_ref=terms_ref.at[to],
                    dst_ref=got_ref.at[step - 1],
                    send_sem=gsend_sem.at[group, step - 1],
                    recv_sem=grecv_sem.at[group, step - 1],
                    device_id={"src": to},
                    device_id_type=MESH,
                )
            )
        return copies

    fwd_load.wait()
    for l in range(layers):
        terms(0, r3_ref, g_red, l, l)
    red_copies = grad_copies(0, g_red, got_red)
    for copy in red_copies:
        copy.start()

    def emit(l):
        pi = red_odd(l)
        for c in range(2):
            red = r3_ref[l, c, PAD : PAD + half, :]
            black = b0_ref[l, c, PAD : PAD + half, :]
            adj_ref[0, c, l, even, :] = jnp.where(pi, black, red)
            adj_ref[0, c, l, odd, :] = jnp.where(pi, red, black)

    for side in range(2):
        halo_sent(0, b0_ref, side)
    for l in range(1, last):
        update(1, 3, r3_ref, b0_ref, PAD, l)
        terms(1, b0_ref, g_in, l, l - 1)
    in_copies = grad_copies(1, g_in, got_in)
    for copy in in_copies:
        copy.start()
    for l in range(1, last):
        emit(l)
    for side in range(2):
        halo_wait(3, r3_ref, side)
    for slot, l in enumerate((0, last)):
        update(1, 3, r3_ref, b0_ref, PAD, l)
        terms(1, b0_ref, g_out, l, slot)
    out_copies = grad_copies(2, g_out, got_out)
    for copy in out_copies:
        copy.start()
    for l in (0, last):
        emit(l)

    for h, buf in ((1, r1_ref), (2, b2_ref), (3, r3_ref)):
        for side in range(2):
            halo_sent(h, buf, side)

    def summed(terms_ref, got_ref, slot):
        value = terms_ref[me, slot]
        for step in range(srcs - 1):
            value = value + got_ref[step, slot]
        return value

    def finish(l, black_ref, got_black, slot):
        pi = red_odd(l)
        red = summed(g_red, got_red, l)
        black = summed(black_ref, got_black, slot)
        grad_ref[l, pl.ds(0, chunk, stride=2), :] = jnp.where(pi, black, red)
        grad_ref[l, pl.ds(1, chunk, stride=2), :] = jnp.where(pi, red, black)

    for copy in red_copies:
        copy.wait()
    for copy in in_copies:
        copy.wait()
    for l in range(1, last):
        finish(l, g_in, got_in, l - 1)
    for copy in out_copies:
        copy.wait()
    for slot, l in enumerate((0, last)):
        finish(l, g_out, got_out, slot)


def body(
    forward_field,
    adjoint_guess,
    conductivity,
    freq_kappa,
    pair_freq,
    recv_data,
    recv_weights,
    recv_x,
    recv_y,
    recv_z,
):
    pair_count, parts, layers, size_y, size_z = adjoint_guess.shape
    assert pair_count == 1
    tiles = lax.axis_size("tile")
    srcs = lax.axis_size("src")
    half = size_y // 2
    chunk = half // srcs
    recv_count = recv_x.shape[0]
    field = (layers, parts, half + 2 * PAD, size_z)
    coef = (2, layers, half, size_z)
    vmem = pl.BlockSpec(memory_space=pltpu.VMEM)
    smem = pl.BlockSpec(memory_space=pltpu.SMEM)
    hbm = pl.BlockSpec(memory_space=pl.ANY)

    def grads(count, depth):
        return pltpu.VMEM((count, depth, chunk, size_z), F32)

    return pl.pallas_call(
        functools.partial(kernel, tiles, srcs),
        out_shape=(
            jax.ShapeDtypeStruct(adjoint_guess.shape, F32),
            jax.ShapeDtypeStruct((layers, size_y // srcs, size_z), F32),
        ),
        in_specs=[smem, smem, hbm, hbm, hbm, vmem, vmem, vmem, vmem, vmem],
        out_specs=(vmem, vmem),
        scratch_shapes=[
            pltpu.VMEM((parts, layers, size_y, size_z), F32),
            pltpu.VMEM((parts, layers, size_y, size_z), F32),
            pltpu.VMEM((layers, size_y, size_z), F32),
            pltpu.VMEM(field, F32),
            pltpu.VMEM(field, F32),
            pltpu.VMEM(field, F32),
            pltpu.VMEM(field, F32),
            pltpu.VMEM((4, 2, parts, half, size_z), F32),
            pltpu.VMEM((2, layers, parts, half, size_z), F32),
            pltpu.VMEM(coef, F32),
            pltpu.VMEM(coef, F32),
            pltpu.VMEM((size_y, 4 * recv_count), BF16),
            pltpu.VMEM((2, 2 * size_z, 4 * recv_count), BF16),
            grads(srcs, layers),
            grads(srcs, layers - 2),
            grads(srcs, 2),
            grads(srcs - 1, layers),
            grads(srcs - 1, layers - 2),
            grads(srcs - 1, 2),
            pltpu.SemaphoreType.DMA((5,)),
            pltpu.SemaphoreType.DMA((4, 2)),
            pltpu.SemaphoreType.DMA((4, 2)),
            pltpu.SemaphoreType.DMA((3, srcs - 1)),
            pltpu.SemaphoreType.DMA((3, srcs - 1)),
        ],
        compiler_params=pltpu.CompilerParams(
            collective_id=0, has_side_effects=True, vmem_limit_bytes=40 << 20
        ),
    )(
        pair_freq,
        freq_kappa,
        forward_field,
        adjoint_guess,
        conductivity,
        recv_data[0],
        recv_weights,
        recv_x[None],
        recv_y[None],
        recv_z[None],
    )


def solution(mesh):
    placed = (
        P(("job", "src"), None, "tile", None, None),
        P(("job", "src"), None, "tile", None, None),
        P(("job", "tile"), None, None),
        P("job"),
        P(("job", "src")),
        P(("job", "src"), None, None),
        P("job", None),
        P("job"),
        P("job"),
        P("job"),
    )
    return jax.shard_map(
        body,
        mesh=mesh,
        in_specs=placed,
        out_specs=(P(("job", "src"), None, "tile", None, None), P(("job", "tile"), "src", None)),
        check_vma=False,
    )
```

time: 114 us -> 33.7 us (0.30)
  waiting for transfers between devices: 37.7 us -> 0 us
  starting transfers between devices: 26.1 us -> 0 us
  Pallas kernels: 0 us -> 25.9 us
  between operations: 15.1 us -> 1.38 us
  matrix products: 11.9 us -> 0 us
  other arithmetic: 11 us -> 0 us
  local copies, waits for them, and re-layouts: 9.25 us -> 6.09 us
  loops' own time: 2.83 us -> 0 us
    ppermute x8 -> x0, starting transfers between devices: 26 us -> none  [the longest x4 20.9 us: with_halo(): lax.ppermute(tail, axis, [(i, (i + 1) % count) for i in range(ends)])]
    pallas_call x0 -> x1, Pallas kernels: none -> 25.9 us  [body(): pl.pallas_call(functools.partial(kernel, tiles, srcs), out_shape=(jax.Sha...]
    reduce_scatter x1 -> x0, waiting for transfers between devices: 24.8 us -> none  [body(): lax.psum_scatter(partial_terms, 'src', scatter_dimension=1, tiled=True)]
    ppermute x8 -> x0, waiting for transfers between devices: 12.9 us -> none  [the longest x4 9.05 us: with_halo(): lax.ppermute(head, axis, [((i + 1) % count, i) for i in range(ends)])]
    dot_general x8 -> x0, matrix products: 11.9 us -> none  [the longest x4 7.46 us: one_layer(): jnp.einsum('rbk,rkz->rbz', plane, col_match, precision=lax.Precision.HIGH...]
    unnamed x20 -> x19, local copies, waits for them, and re-layouts: 0.95 us -> 6.09 us
    add x8 -> x0, other arithmetic: 3.7 us -> none  [the longest x4 3.52 us: neighbour_update(): sums = source + beside_all]
    another operation x4 -> x0, other arithmetic: 3.43 us -> none  [neighbour_update(): jnp.stack([real_part, imag_part], axis=1)]
  transfers between devices with their start and end apart: 9 -> 0, of which waited for: 7 -> 0; matrix products, arithmetic and copies ran while one was open for 17% -> 0% of each run, Pallas kernels for 0% -> 0%
where the time goes in v1:
time: 33.7 us; the launch traced here: 33.4 us
  Pallas kernels  25.9 us (77%)
  local copies, waits for them, and re-layouts  6.09 us (18%)
  between operations  1.38 us (4%)
    pallas_call x1, Pallas kernels, body(): pl.pallas_call(functools.partial(kernel, tiles, srcs), out_shape=(jax.Sha...  25.9 us
    unnamed x19, local copies, waits for them, and re-layouts  6.09 us

profile of v1, /device:TPU:0, one launch (start us, length us, event | category | flops | bytes accessed | tf_op | source)
XLA Modules:
  0.0 33.4 jit_solution(12941975870668256744)
XLA Ops:
  1.3 0.0 copy-start.3
  1.3 0.0 copy-start.4
  1.3 0.0 copy-start.5
  1.3 0.0 copy-start.6
  1.3 0.0 copy-start.7
  1.3 1.0 %copy.12.weights_ref = f32[256,64]{1,0:T(8,128)S(1)} copy(f32[256,64]{0,1:T(8,128)} %param.16) | data formatting | bytes 131072 | tf_op args[6]
  2.3 0.0 copy-done.3
  2.3 0.0 copy-done.4
  2.3 0.0 copy-done.5
  2.3 0.0 copy-done.6
  2.3 0.0 copy-done.7
  2.3 0.0 copy-start
  2.4 1.2 %copy-done = f32[1,2,4,256,128]{4,3,2,1,0:T(8,128)S(1)} copy-done((f32[1,2,4,256,128]{4,3,2,1,0:T(8,128)S(1)}, f32[1,2,4,256,128]{4,3,2,1,0:T(8,128)}, u32[]{:S(2)}) %copy-start) | copy-done | bytes 1048600
  3.6 0.0 copy-start.1
  3.6 1.2 %copy-done.1 = f32[1,2,4,256,128]{4,3,2,1,0:T(8,128)S(1)} copy-done((f32[1,2,4,256,128]{4,3,2,1,0:T(8,128)S(1)}, f32[1,2,4,256,128]{4,3,2,1,0:T(8,128)}, u32[]{:S(2)}) %copy-start.1) | copy-done | bytes 1048600
  4.8 0.0 copy-start.2
  4.8 1.0 %copy-done.2 = f32[4,256,128]{2,1,0:T(8,128)S(1)} copy-done((f32[4,256,128]{2,1,0:T(8,128)S(1)}, f32[4,256,128]{2,1,0:T(8,128)}, u32[]{:S(2)}) %copy-start.2) | copy-done | bytes 524312
  5.8 25.9 %shard_map.113 = (f32[1,2,4,256,128]{4,3,2,1,0:T(8,128)S(1)}, f32[4,64,128]{2,1,0:T(8,128)S(1)}) custom-call(s32[1]{0:T(128)S(6)} %copy.15.freq_ref, f32[4]{0:T(128)S(1)} %copy-done.7, f32[1,2,4,256,128]{4,3,2,1,0:T(8,128)S(1)} %copy-done, f32[1,2,4,256,128]{4,3,2,1,0:T(8,128)S(1)} %copy-done.1, f32[4,256,128]{2,1,0:T(8,128)S(1)} %copy-done.2, ...), custom_call_target="tpu_custom_call" | custom-call | tf_op jit(solution)/shard_map/pallas_call | solution.py:390
  31.8 1.0 %copy.16 = f32[1,2,4,256,128]{4,3,2,1,0:T(8,128)} copy(f32[1,2,4,256,128]{4,3,2,1,0:T(8,128)S(1)} %get-tuple-element.4) | data formatting | bytes 2097152
  32.7 0.7 %copy.17 = f32[4,64,128]{2,1,0:T(8,128)} copy(f32[4,64,128]{2,1,0:T(8,128)S(1)} %get-tuple-element.5) | data formatting | bytes 262144
Async XLA Ops:
  1.3 1.0 %copy-start.3 = (f32[1,2,256]{2,1,0:T(2,128)S(1)}, f32[1,2,256]{2,1,0:T(2,128)}, u32[]{:S(2)}) copy-start(f32[1,2,256]{2,1,0:T(2,128)} %param.15) | copy-start | bytes 6148
  1.3 1.0 %copy-start.4 = (s32[256]{0:T(256)S(1)}, s32[256]{0:T(256)}, u32[]{:S(2)}) copy-start(s32[256]{0:T(256)} %param.17) | copy-start | bytes 3076
  1.3 1.0 %copy-start.5 = (s32[256]{0:T(256)S(1)}, s32[256]{0:T(256)}, u32[]{:S(2)}) copy-start(s32[256]{0:T(256)} %param.18) | copy-start | bytes 3076
  1.3 1.0 %copy-start.6 = (s32[256]{0:T(256)S(1)}, s32[256]{0:T(256)}, u32[]{:S(2)}) copy-start(s32[256]{0:T(256)} %param.19) | copy-start | bytes 3076
  1.3 1.0 %copy-start.7 = (f32[4]{0:T(128)S(1)}, f32[4]{0:T(128)}, u32[]{:S(2)}) copy-start(f32[4]{0:T(128)} %kappa_ref.1) | copy-start | bytes 52
  2.3 1.2 %copy-start = (f32[1,2,4,256,128]{4,3,2,1,0:T(8,128)S(1)}, f32[1,2,4,256,128]{4,3,2,1,0:T(8,128)}, u32[]{:S(2)}) copy-start(f32[1,2,4,256,128]{4,3,2,1,0:T(8,128)} %fwd_hbm.1) | copy-start | bytes 3145732
  3.6 1.2 %copy-start.1 = (f32[1,2,4,256,128]{4,3,2,1,0:T(8,128)S(1)}, f32[1,2,4,256,128]{4,3,2,1,0:T(8,128)}, u32[]{:S(2)}) copy-start(f32[1,2,4,256,128]{4,3,2,1,0:T(8,128)} %guess_hbm.1) | copy-start | bytes 3145732
  4.8 1.0 %copy-start.2 = (f32[4,256,128]{2,1,0:T(8,128)S(1)}, f32[4,256,128]{2,1,0:T(8,128)}, u32[]{:S(2)}) copy-start(f32[4,256,128]{2,1,0:T(8,128)} %cond_hbm.1) | copy-start | bytes 1572868

commit v2 on v1

--- a/solution.py
+++ b/solution.py
@@ -125,31 +125,32 @@
                 pi, guess_ref[c, l, even, :], guess_ref[c, l, odd, :]
             )
 
-    def halo_copy(h, buf, side):
+    def halo_copy(h, buf, side, s):
         l, to = (last, right) if side == 0 else (0, left)
         return pltpu.make_async_remote_copy(
-            src_ref=buf.at[l, :, pl.ds(PAD, half), :],
-            dst_ref=halo_ref.at[h, side],
-            send_sem=send_sem.at[h, side],
-            recv_sem=recv_sem.at[h, side],
+            src_ref=buf.at[l, :, pl.ds(PAD + s * chunk, chunk), :],
+            dst_ref=halo_ref.at[h, side, :, pl.ds(s * chunk, chunk), :],
+            send_sem=send_sem.at[h, side, s],
+            recv_sem=recv_sem.at[h, side, s],
             device_id={"tile": to},
             device_id_type=MESH,
         )
 
-    def halo_start(h, buf, side):
+    def halo_start(h, buf, side, s):
         @pl.when(has_right if side == 0 else has_left)
         def _():
-            halo_copy(h, buf, side).start()
-
-    def halo_wait(h, buf, side):
+            halo_copy(h, buf, side, s).start()
+
+    def halo_wait(h, buf, side, s):
         @pl.when(has_left if side == 0 else has_right)
         def _():
-            halo_copy(h, buf, side).wait_recv()
+            halo_copy(h, buf, side, s).wait_recv()
 
     def halo_sent(h, buf, side):
         @pl.when(has_right if side == 0 else has_left)
         def _():
-            halo_copy(h, buf, side).wait_send()
+            for s in range(srcs):
+                halo_copy(h, buf, side, s).wait_send()
 
     for copy, l in zip(edge_loads, (0, last)):
         copy.wait()
@@ -158,8 +159,9 @@
     peers = has_left.astype(jnp.int32) + has_right.astype(jnp.int32) + (srcs - 1)
     pl.semaphore_wait(barrier, peers)
 
-    for side in range(2):
-        halo_start(0, b0_ref, side)
+    for s in range(srcs):
+        for side in range(2):
+            halo_start(0, b0_ref, side, s)
 
     cond_load.wait()
     freq = freq_ref[0]
@@ -186,7 +188,7 @@
             rows_ref[parity * half : (parity + 1) * half, b * recv_count : (b + 1) * recv_count] = (
                 jnp.where(row + parity == ry + b, 1.0, 0.0).astype(BF16)
             )
-    w_t = jnp.transpose(weights_ref[...])
+    w_t = weights_ref[...]
     rx = rx_ref[...]
     rz = rz_ref[...]
     ZC = 16
@@ -220,55 +222,52 @@
             src_ref[0, l, c] = jnp.where(pi, so, se)
             src_ref[1, l, c] = jnp.where(pi, se, so)
 
-    RC = min(32, half)
-
-    def update(colour, h, buf, out, out_pad, l):
+    def update(colour, h, buf, out, out_pad, l, pieces):
         up_side = red_odd(l) if colour == 0 else jnp.logical_not(red_odd(l))
-        for r in range(0, half, RC):
+        for r in (chunk * s for s in pieces):
             sums = []
             for c in range(2):
-                mid = buf[l, c, PAD + r : PAD + r + RC, :]
-                s = src_ref[colour, l, c, r : r + RC, :] + mid
+                mid = buf[l, c, PAD + r : PAD + r + chunk, :]
+                s = src_ref[colour, l, c, r : r + chunk, :] + mid
                 s = s + jnp.where(
                     up_side,
-                    buf[l, c, PAD + r + 1 : PAD + r + 1 + RC, :],
-                    buf[l, c, PAD + r - 1 : PAD + r - 1 + RC, :],
+                    buf[l, c, PAD + r + 1 : PAD + r + 1 + chunk, :],
+                    buf[l, c, PAD + r - 1 : PAD + r - 1 + chunk, :],
                 )
                 if l == 0:
-                    s = s + halo_ref[h, 0, c, r : r + RC, :]
+                    s = s + halo_ref[h, 0, c, r : r + chunk, :]
                 else:
-                    s = s + buf[l - 1, c, PAD + r : PAD + r + RC, :]
+                    s = s + buf[l - 1, c, PAD + r : PAD + r + chunk, :]
                 if l == last:
-                    s = s + halo_ref[h, 1, c, r : r + RC, :]
+                    s = s + halo_ref[h, 1, c, r : r + chunk, :]
                 else:
-                    s = s + buf[l + 1, c, PAD + r : PAD + r + RC, :]
+                    s = s + buf[l + 1, c, PAD + r : PAD + r + chunk, :]
                 s = s + jnp.where(lane == 0, 0.0, pltpu.roll(mid, 1, 1))
                 s = s + jnp.where(lane == size_z - 1, 0.0, pltpu.roll(mid, size_z - 1, 1))
                 sums.append(s)
-            c6 = c6_ref[colour, l, r : r + RC, :]
-            cc = cc_ref[colour, l, r : r + RC, :]
-            out[l, 0, out_pad + r : out_pad + r + RC, :] = c6 * sums[0] + cc * sums[1]
-            out[l, 1, out_pad + r : out_pad + r + RC, :] = c6 * sums[1] - cc * sums[0]
+            c6 = c6_ref[colour, l, r : r + chunk, :]
+            cc = cc_ref[colour, l, r : r + chunk, :]
+            out[l, 0, out_pad + r : out_pad + r + chunk, :] = c6 * sums[0] + cc * sums[1]
+            out[l, 1, out_pad + r : out_pad + r + chunk, :] = c6 * sums[1] - cc * sums[0]
+
+    every = range(srcs)
 
     def sweep(colour, h, buf, out):
         for l in range(1, last):
-            update(colour, h, buf, out, PAD, l)
-        for side in range(2):
-            halo_wait(h, buf, side)
-        update(colour, h, buf, out, PAD, last)
-        if h < 3:
-            halo_start(h + 1, out, 0)
-        update(colour, h, buf, out, PAD, 0)
-        if h < 3:
-            halo_start(h + 1, out, 1)
+            update(colour, h, buf, out, PAD, l, every)
+        for s in every:
+            for side, l in ((0, 0), (1, last)):
+                halo_wait(h, buf, side, s)
+                update(colour, h, buf, out, PAD, l, (s,))
+                halo_start(h + 1, out, 1 - side, s)
 
     sweep(0, 0, b0_ref, r1_ref)
     sweep(1, 1, r1_ref, b2_ref)
     sweep(0, 2, b2_ref, r3_ref)
 
-    def terms(colour, buf, out, l, slot):
+    def terms(colour, buf, out, l, slot, pieces):
         pi = red_odd(l) if colour == 0 else jnp.logical_not(red_odd(l))
-        for s in range(srcs):
+        for s in pieces:
             e = pl.ds(2 * s * chunk, chunk, stride=2)
             o = pl.ds(2 * s * chunk + 1, chunk, stride=2)
             fre = jnp.where(pi, fwd_ref[0, l, o, :], fwd_ref[0, l, e, :])
@@ -296,7 +295,7 @@
 
     fwd_load.wait()
     for l in range(layers):
-        terms(0, r3_ref, g_red, l, l)
+        terms(0, r3_ref, g_red, l, l, every)
     red_copies = grad_copies(0, g_red, got_red)
     for copy in red_copies:
         copy.start()
@@ -312,21 +311,35 @@
     for side in range(2):
         halo_sent(0, b0_ref, side)
     for l in range(1, last):
-        update(1, 3, r3_ref, b0_ref, PAD, l)
-        terms(1, b0_ref, g_in, l, l - 1)
+        update(1, 3, r3_ref, b0_ref, PAD, l, every)
+        terms(1, b0_ref, g_in, l, l - 1, every)
     in_copies = grad_copies(1, g_in, got_in)
     for copy in in_copies:
         copy.start()
     for l in range(1, last):
         emit(l)
-    for side in range(2):
-        halo_wait(3, r3_ref, side)
-    for slot, l in enumerate((0, last)):
-        update(1, 3, r3_ref, b0_ref, PAD, l)
-        terms(1, b0_ref, g_out, l, slot)
+    def out_copy(s):
+        step = lax.rem(s - me + srcs - 1, srcs)
+        return pltpu.make_async_remote_copy(
+            src_ref=g_out.at[s],
+            dst_ref=got_out.at[step],
+            send_sem=gsend_sem.at[2, step],
+            recv_sem=grecv_sem.at[2, step],
+            device_id={"src": s},
+            device_id_type=MESH,
+        )
+
+    for s in every:
+        for side, l in ((0, 0), (1, last)):
+            halo_wait(3, r3_ref, side, s)
+            update(1, 3, r3_ref, b0_ref, PAD, l, (s,))
+            terms(1, b0_ref, g_out, l, side, (s,))
+
+        @pl.when(me != s)
+        def _():
+            out_copy(s).start()
+
     out_copies = grad_copies(2, g_out, got_out)
-    for copy in out_copies:
-        copy.start()
     for l in (0, last):
         emit(l)
 
@@ -382,12 +395,12 @@
     coef = (2, layers, half, size_z)
     vmem = pl.BlockSpec(memory_space=pltpu.VMEM)
     smem = pl.BlockSpec(memory_space=pltpu.SMEM)
-    hbm = pl.BlockSpec(memory_space=pl.ANY)
+    hbm = pl.BlockSpec(memory_space=pltpu.HBM)
 
     def grads(count, depth):
         return pltpu.VMEM((count, depth, chunk, size_z), F32)
 
-    return pl.pallas_call(
+    results = pl.pallas_call(
         functools.partial(kernel, tiles, srcs),
         out_shape=(
             jax.ShapeDtypeStruct(adjoint_guess.shape, F32),
@@ -416,13 +429,13 @@
             grads(srcs - 1, layers - 2),
             grads(srcs - 1, 2),
             pltpu.SemaphoreType.DMA((5,)),
-            pltpu.SemaphoreType.DMA((4, 2)),
-            pltpu.SemaphoreType.DMA((4, 2)),
+            pltpu.SemaphoreType.DMA((4, 2, srcs)),
+            pltpu.SemaphoreType.DMA((4, 2, srcs)),
             pltpu.SemaphoreType.DMA((3, srcs - 1)),
             pltpu.SemaphoreType.DMA((3, srcs - 1)),
         ],
         compiler_params=pltpu.CompilerParams(
-            collective_id=0, has_side_effects=True, vmem_limit_bytes=40 << 20
+            collective_id=0, has_side_effects=True, vmem_limit_bytes=58 << 20
         ),
     )(
         pair_freq,
@@ -431,11 +444,12 @@
         adjoint_guess,
         conductivity,
         recv_data[0],
-        recv_weights,
+        recv_weights.T,
         recv_x[None],
         recv_y[None],
         recv_z[None],
     )
+    return results
 
 
 def solution(mesh):

time: 33.7 us -> 27.8 us (0.82)
  local copies, waits for them, and re-layouts: 6.09 us -> 2.96 us
  Pallas kernels: 25.9 us -> 23.3 us
    unnamed x19 -> x4, local copies, waits for them, and re-layouts: 6.09 us -> 2.96 us
    pallas_call x1, Pallas kernels: 25.9 us -> 23.3 us  [body(): pl.pallas_call(functools.partial(kernel, tiles, srcs), out_shape=(jax.Sha...]
where the time goes in v2:
time: 27.8 us; the launch traced here: 27.6 us
  Pallas kernels  23.3 us (84%)
  local copies, waits for them, and re-layouts  2.96 us (11%)
  between operations  1.3 us (5%)
    pallas_call x1, Pallas kernels, body(): pl.pallas_call(functools.partial(kernel, tiles, srcs), out_shape=(jax.Sha...  23.3 us
    unnamed x4, local copies, waits for them, and re-layouts  2.96 us

profile of v2, /device:TPU:0, one launch (start us, length us, event | category | flops | bytes accessed | tf_op | source)
XLA Modules:
  0.0 27.6 jit_solution(10835356881119586341)
XLA Ops:
  1.3 23.3 %shard_map.113 = (f32[1,2,4,256,128]{4,3,2,1,0:T(8,128)}, f32[4,64,128]{2,1,0:T(8,128)}) custom-call(s32[1]{0:T(128)S(6)} %copy.14.freq_ref, f32[4]{0:T(128)} %kappa_ref.1, f32[1,2,4,256,128]{4,3,2,1,0:T(8,128)} %fwd_hbm.1, f32[1,2,4,256,128]{4,3,2,1,0:T(8,128)} %guess_hbm.1, f32[4,256,128]{2,1,0:T(8,128)} %cond_hbm.1, f32[2,256]{1,0:T(2,128)} %bitcast.6, ...), custom_call_target="tpu_custom_call" | custom-call | tf_op jit(solution)/shard_map/pallas_call | solution.py:403
  24.6 0.0 copy-start
  24.6 2.3 %copy.15 = f32[1,2,4,256,128]{4,3,2,1,0:T(8,128)} copy(f32[1,2,4,256,128]{4,3,2,1,0:T(8,128)} %get-tuple-element.4) | data formatting | bytes 2097152
  26.9 0.0 copy-done
  26.9 0.7 %copy.16 = f32[4,64,128]{2,1,0:T(8,128)} copy(f32[4,64,128]{2,1,0:T(8,128)S(1)} %copy-done) | data formatting | bytes 262144
Async XLA Ops:
  24.6 2.3 %copy-start = (f32[4,64,128]{2,1,0:T(8,128)S(1)}, f32[4,64,128]{2,1,0:T(8,128)}, u32[]{:S(2)}) copy-start(f32[4,64,128]{2,1,0:T(8,128)} %get-tuple-element.5) | copy-start | bytes 393220

commit v3 on v2

--- a/solution.py
+++ b/solution.py
@@ -42,9 +42,11 @@
     rows_ref,
     cols_ref,
     g_red,
+    g_rim,
     g_in,
     g_out,
     got_red,
+    got_rim,
     got_in,
     got_out,
     load_sem,
@@ -252,9 +254,10 @@
 
     every = range(srcs)
 
-    def sweep(colour, h, buf, out):
+    def sweep(colour, h, buf, out, between=lambda: None):
         for l in range(1, last):
             update(colour, h, buf, out, PAD, l, every)
+        between()
         for s in every:
             for side, l in ((0, 0), (1, last)):
                 halo_wait(h, buf, side, s)
@@ -263,7 +266,6 @@
 
     sweep(0, 0, b0_ref, r1_ref)
     sweep(1, 1, r1_ref, b2_ref)
-    sweep(0, 2, b2_ref, r3_ref)
 
     def terms(colour, buf, out, l, slot, pieces):
         pi = red_odd(l) if colour == 0 else jnp.logical_not(red_odd(l))
@@ -293,11 +295,20 @@
             )
         return copies
 
-    fwd_load.wait()
-    for l in range(layers):
-        terms(0, r3_ref, g_red, l, l, every)
     red_copies = grad_copies(0, g_red, got_red)
-    for copy in red_copies:
+
+    def red_inner():
+        fwd_load.wait()
+        for l in range(1, last):
+            terms(0, r3_ref, g_red, l, l - 1, every)
+        for copy in red_copies:
+            copy.start()
+
+    sweep(0, 2, b2_ref, r3_ref, red_inner)
+    for slot, l in enumerate((0, last)):
+        terms(0, r3_ref, g_rim, l, slot, every)
+    rim_copies = grad_copies(3, g_rim, got_rim)
+    for copy in rim_copies:
         copy.start()
 
     def emit(l):
@@ -353,9 +364,9 @@
             value = value + got_ref[step, slot]
         return value
 
-    def finish(l, black_ref, got_black, slot):
+    def finish(l, red_ref, got_red, black_ref, got_black, slot):
         pi = red_odd(l)
-        red = summed(g_red, got_red, l)
+        red = summed(red_ref, got_red, slot)
         black = summed(black_ref, got_black, slot)
         grad_ref[l, pl.ds(0, chunk, stride=2), :] = jnp.where(pi, black, red)
         grad_ref[l, pl.ds(1, chunk, stride=2), :] = jnp.where(pi, red, black)
@@ -365,11 +376,27 @@
     for copy in in_copies:
         copy.wait()
     for l in range(1, last):
-        finish(l, g_in, got_in, l - 1)
+        finish(l, g_red, got_red, g_in, got_in, l - 1)
+    for copy in rim_copies:
+        copy.wait()
     for copy in out_copies:
         copy.wait()
     for slot, l in enumerate((0, last)):
-        finish(l, g_out, got_out, slot)
+        finish(l, g_rim, got_rim, g_out, got_out, slot)
+
+
+def store_kernel(adj_ref, grad_ref, adj_hbm, grad_hbm, sem):
+    parts, layers = adj_ref.shape[1:3]
+    copies = [pltpu.make_async_copy(grad_ref, grad_hbm, sem.at[0])]
+    for c in range(parts):
+        for l in range(layers):
+            copies.append(
+                pltpu.make_async_copy(adj_ref.at[0, c, l], adj_hbm.at[0, c, l], sem.at[len(copies)])
+            )
+    for copy in copies:
+        copy.start()
+    for copy in copies:
+        copy.wait()
 
 
 def body(
@@ -422,34 +449,44 @@
             pltpu.VMEM(coef, F32),
             pltpu.VMEM((size_y, 4 * recv_count), BF16),
             pltpu.VMEM((2, 2 * size_z, 4 * recv_count), BF16),
-            grads(srcs, layers),
             grads(srcs, layers - 2),
             grads(srcs, 2),
-            grads(srcs - 1, layers),
+            grads(srcs, layers - 2),
+            grads(srcs, 2),
+            grads(srcs - 1, layers - 2),
+            grads(srcs - 1, 2),
             grads(srcs - 1, layers - 2),
             grads(srcs - 1, 2),
             pltpu.SemaphoreType.DMA((5,)),
             pltpu.SemaphoreType.DMA((4, 2, srcs)),
             pltpu.SemaphoreType.DMA((4, 2, srcs)),
-            pltpu.SemaphoreType.DMA((3, srcs - 1)),
-            pltpu.SemaphoreType.DMA((3, srcs - 1)),
+            pltpu.SemaphoreType.DMA((4, srcs - 1)),
+            pltpu.SemaphoreType.DMA((4, srcs - 1)),
         ],
         compiler_params=pltpu.CompilerParams(
-            collective_id=0, has_side_effects=True, vmem_limit_bytes=58 << 20
+            collective_id=0, has_side_effects=True, vmem_limit_bytes=40 << 20
         ),
     )(
         pair_freq,
         freq_kappa,
-        forward_field,
-        adjoint_guess,
-        conductivity,
+        *(
+            pltpu.with_memory_space_constraint(a, pltpu.HBM)
+            for a in (forward_field, adjoint_guess, conductivity)
+        ),
         recv_data[0],
         recv_weights.T,
         recv_x[None],
         recv_y[None],
         recv_z[None],
     )
-    return results
+    return pl.pallas_call(
+        store_kernel,
+        out_shape=tuple(jax.ShapeDtypeStruct(r.shape, F32) for r in results),
+        in_specs=[vmem, vmem],
+        out_specs=(hbm, hbm),
+        scratch_shapes=[pltpu.SemaphoreType.DMA((1 + parts * layers,))],
+        compiler_params=pltpu.CompilerParams(vmem_limit_bytes=2 << 20),
+    )(*results)
 
 
 def solution(mesh):

time: 27.8 us -> 25.7 us (0.924)
  local copies, waits for them, and re-layouts: 2.96 us -> 1.53 us
  Pallas kernels: 23.3 us -> 22.6 us
    pallas_call x1, Pallas kernels: 23.3 us -> 21.6 us  [body(): pl.pallas_call(functools.partial(kernel, tiles, srcs), out_shape=(jax.Sha...]
    unnamed x4 -> x12, local copies, waits for them, and re-layouts: 2.96 us -> 1.53 us
    pallas_call x0 -> x1, Pallas kernels: none -> 1.08 us  [body(): pl.pallas_call(store_kernel, out_shape=tuple((jax.ShapeDtypeStruct(r.shap...]
where the time goes in v3:
time: 25.7 us; the launch traced here: 25.5 us
  Pallas kernels  22.6 us (88%)
  local copies, waits for them, and re-layouts  1.53 us (6%)
  between operations  1.33 us (5%)
    pallas_call x1, Pallas kernels, body(): pl.pallas_call(functools.partial(kernel, tiles, srcs), out_shape=(jax.Sha...  21.6 us
    unnamed x12, local copies, waits for them, and re-layouts  1.53 us
    pallas_call x1, Pallas kernels, body(): pl.pallas_call(store_kernel, out_shape=tuple((jax.ShapeDtypeStruct(r.shap...  1.08 us

profile of v3, /device:TPU:0, one launch (start us, length us, event | category | flops | bytes accessed | tf_op | source)
XLA Modules:
  0.0 25.5 jit_solution(7535124137118639315)
XLA Ops:
  1.3 0.0 copy-start.3
  1.3 0.0 copy-start.4
  1.3 0.0 copy-start.1
  1.3 0.0 copy-start.2
  1.3 0.0 copy-start.5
  1.3 0.6 %copy-done.3 = s32[256]{0:T(256)S(1)} copy-done((s32[256]{0:T(256)S(1)}, s32[256]{0:T(256)}, u32[]{:S(2)}) %copy-start.3) | copy-done | bytes 1048
  2.0 0.0 copy-done.4
  2.0 0.0 copy-done.1
  2.0 0.0 copy-done.2
  2.0 0.0 copy-done.5
  2.0 0.0 copy-start
  2.0 0.8 %copy-done = f32[256,64]{0,1:T(8,128)S(1)} copy-done((f32[256,64]{0,1:T(8,128)S(1)}, f32[256,64]{0,1:T(8,128)}, u32[]{:S(2)}) %copy-start) | copy-done | bytes 65560
  2.9 21.6 %shard_map.113 = (f32[1,2,4,256,128]{4,3,2,1,0:T(8,128)S(1)}, f32[4,64,128]{2,1,0:T(8,128)S(1)}) custom-call(s32[1]{0:T(128)S(6)} %copy.12.freq_ref, f32[4]{0:T(128)S(1)} %copy-done.5, f32[1,2,4,256,128]{4,3,2,1,0:T(8,128)} %fwd_hbm.1, f32[1,2,4,256,128]{4,3,2,1,0:T(8,128)} %guess_hbm.1, f32[4,256,128]{2,1,0:T(8,128)} %cond_hbm.1, f32[2,256]{1,0:T(2,128)S(1)} %bitcast.6, ...), custom_call_target="tpu_custom_call" | custom-call | tf_op jit(solution)/shard_map/pallas_call | solution.py:430
  24.4 1.1 %shard_map.114 = (f32[1,2,4,256,128]{4,3,2,1,0:T(8,128)}, f32[4,64,128]{2,1,0:T(8,128)}) custom-call(f32[1,2,4,256,128]{4,3,2,1,0:T(8,128)S(1)} %get-tuple-element.4.adj_ref, f32[4,64,128]{2,1,0:T(8,128)S(1)} %get-tuple-element.5.grad_ref), custom_call_target="tpu_custom_call" | custom-call | tf_op jit(solution)/shard_map/pallas_call | solution.py:482
Async XLA Ops:
  1.3 0.7 %copy-start.3 = (s32[256]{0:T(256)S(1)}, s32[256]{0:T(256)}, u32[]{:S(2)}) copy-start(s32[256]{0:T(256)} %param.18) | copy-start | bytes 3076
  1.3 0.7 %copy-start.4 = (s32[256]{0:T(256)S(1)}, s32[256]{0:T(256)}, u32[]{:S(2)}) copy-start(s32[256]{0:T(256)} %param.19) | copy-start | bytes 3076
  1.3 0.7 %copy-start.1 = (f32[1,2,256]{2,1,0:T(2,128)S(1)}, f32[1,2,256]{2,1,0:T(2,128)}, u32[]{:S(2)}) copy-start(f32[1,2,256]{2,1,0:T(2,128)} %param.15) | copy-start | bytes 6148
  1.3 0.7 %copy-start.2 = (s32[256]{0:T(256)S(1)}, s32[256]{0:T(256)}, u32[]{:S(2)}) copy-start(s32[256]{0:T(256)} %param.17) | copy-start | bytes 3076
  1.3 0.7 %copy-start.5 = (f32[4]{0:T(128)S(1)}, f32[4]{0:T(128)}, u32[]{:S(2)}) copy-start(f32[4]{0:T(128)} %kappa_ref.1) | copy-start | bytes 52
  2.0 0.8 %copy-start = (f32[256,64]{0,1:T(8,128)S(1)}, f32[256,64]{0,1:T(8,128)}, u32[]{:S(2)}) copy-start(f32[256,64]{0,1:T(8,128)} %param.16) | copy-start | bytes 196612

commit v4 on v3

--- a/solution.py
+++ b/solution.py
@@ -471,13 +471,9 @@
         freq_kappa,
         *(
             pltpu.with_memory_space_constraint(a, pltpu.HBM)
-            for a in (forward_field, adjoint_guess, conductivity)
+            for a in (forward_field, adjoint_guess, conductivity, recv_data[0], recv_weights.T)
         ),
-        recv_data[0],
-        recv_weights.T,
-        recv_x[None],
-        recv_y[None],
-        recv_z[None],
+        *(pltpu.with_memory_space_constraint(a[None], pltpu.HBM) for a in (recv_x, recv_y, recv_z)),
     )
     return pl.pallas_call(
         store_kernel,

time: 25.7 us -> 25.1 us (0.977)
  local copies, waits for them, and re-layouts: 1.53 us -> 0.65 us
  Pallas kernels: 22.6 us -> 22.9 us
    unnamed x12 -> x2, local copies, waits for them, and re-layouts: 1.53 us -> 0.65 us
    pallas_call x1, Pallas kernels: 21.6 us -> 21.9 us  [body(): pl.pallas_call(functools.partial(kernel, tiles, srcs), out_shape=(jax.Sha...]
where the time goes in v4:
time: 25.1 us; the launch traced here: 24.9 us
  Pallas kernels  22.9 us (91%)
  between operations  1.3 us (5%)
  local copies, waits for them, and re-layouts  0.65 us (3%)
    pallas_call x1, Pallas kernels, body(): pl.pallas_call(functools.partial(kernel, tiles, srcs), out_shape=(jax.Sha...  21.9 us
    pallas_call x1, Pallas kernels, body(): pl.pallas_call(store_kernel, out_shape=tuple((jax.ShapeDtypeStruct(r.shap...  1.08 us
    unnamed x2, local copies, waits for them, and re-layouts  0.65 us

profile of v4, /device:TPU:0, one launch (start us, length us, event | category | flops | bytes accessed | tf_op | source)
XLA Modules:
  0.0 24.9 jit_solution(14431745206464041128)
XLA Ops:
  1.3 0.0 copy-start
  1.3 0.6 %copy-done = f32[4]{0:T(128)S(1)} copy-done((f32[4]{0:T(128)S(1)}, f32[4]{0:T(128)}, u32[]{:S(2)}) %copy-start) | copy-done | bytes 40
  1.9 21.9 %shard_map.113 = (f32[1,2,4,256,128]{4,3,2,1,0:T(8,128)S(1)}, f32[4,64,128]{2,1,0:T(8,128)S(1)}) custom-call(s32[1]{0:T(128)S(6)} %copy.12.freq_ref, f32[4]{0:T(128)S(1)} %copy-done, f32[1,2,4,256,128]{4,3,2,1,0:T(8,128)} %fwd_hbm.1, f32[1,2,4,256,128]{4,3,2,1,0:T(8,128)} %guess_hbm.1, f32[4,256,128]{2,1,0:T(8,128)} %cond_hbm.1, f32[2,256]{1,0:T(2,128)} %bitcast.6, ...), custom_call_target="tpu_custom_call" | custom-call | tf_op jit(solution)/shard_map/pallas_call | solution.py:430
  23.8 1.1 %shard_map.114 = (f32[1,2,4,256,128]{4,3,2,1,0:T(8,128)}, f32[4,64,128]{2,1,0:T(8,128)}) custom-call(f32[1,2,4,256,128]{4,3,2,1,0:T(8,128)S(1)} %get-tuple-element.4.adj_ref, f32[4,64,128]{2,1,0:T(8,128)S(1)} %get-tuple-element.5.grad_ref), custom_call_target="tpu_custom_call" | custom-call | tf_op jit(solution)/shard_map/pallas_call | solution.py:478
Async XLA Ops:
  1.3 0.7 %copy-start = (f32[4]{0:T(128)S(1)}, f32[4]{0:T(128)}, u32[]{:S(2)}) copy-start(f32[4]{0:T(128)} %kappa_ref.1) | copy-start | bytes 52
